TPU v7x, 128 devices: a whole 4x4x4 slice. The times are simulated.
128 devices in a mesh: row: 8 (over z, core), col: 16 (over y, x).
Axes of the slice: x: 4, y: 4, z: 4, core: 2. Of those that a mesh axis runs over, the one named last changes fastest.
Arguments:
- working: float32 [8, 8, 256, 4, 16, 256], P(None, 'row', None, None, 'col'), may hold values from -6 to 6
- factor_panel: float32 [2, 8, 8, 256, 256], P(None, None, 'row'), may hold values from -0.12 to 2, as said below
Outputs:
- gram_part: float32 [8, 8, 256, 4, 16, 256], P(None, 'row', None, None, 'col')
- finished_columns: float32 [4, 8, 256, 16, 8, 128], P(None, None, None, 'col', 'row')
Inputs may be any that keep to these rules, and one draw needn't show every extreme that they name: factor_panel holds a lower-triangular factor: entries above the factor's diagonal are zero and its diagonal entries lie between 1 and 2.
All inputs are finite; a program needn't handle non-finite values.
Results may differ from a plain program's by a relative error of at most 0.0001.
Values sent between devices are 32-bit elements; how exact they have to be, the bound alone decides.
A program may use at most 192 MiB of HBM per device.

v0:
```python
import jax
import jax.numpy as jnp
from jax import lax
from jax.sharding import PartitionSpec as P

BLK = 256
K = 30
STEPS = 2


def picked(value, axis, root):
    return lax.dynamic_index_in_dim(lax.all_gather(value, axis), root, 0, keepdims=False)


def per_device(working, factor_panel):
    row_count = lax.axis_size("row")
    col_count = lax.axis_size("col")
    row_index = lax.axis_index("row")
    blocks_rows = working.shape[0]
    width = working.shape[2]
    blocks_cols = working.shape[3]
    matrix_rows = working.reshape(blocks_rows, width, blocks_cols * width)
    global_block = jnp.arange(blocks_rows) * row_count + row_index

    def solve_row(slab, step_index):
        target = K + step_index
        owner = target % row_count
        diagonal = jnp.tril(factor_panel[step_index, target // row_count, 0])
        diagonal = jnp.where(row_index == owner, diagonal, jnp.eye(width, dtype=jnp.float32))
        solved = lax.linalg.triangular_solve(diagonal, slab, left_side=True, lower=True)
        return picked(solved, "row", owner)

    def eliminate(rows_part, blocks_part, column_part, solved, step_index):
        target = K + step_index
        updated = rows_part - jnp.einsum(
            "rab,bc->rac", column_part, solved, precision=lax.Precision.HIGHEST
        )
        below = (blocks_part > target)[:, None, None]
        here = (blocks_part == target)[:, None, None]
        return jnp.where(below, updated, jnp.where(here, solved[None], rows_part))

    solved_list = []
    solved = solve_row(matrix_rows[K // row_count], 0)
    for step_index in range(STEPS):
        solved_list.append(solved)
        if step_index + 1 < STEPS:
            slot = (K + step_index + 1) // row_count
            next_slab = eliminate(
                matrix_rows[slot : slot + 1],
                global_block[slot : slot + 1],
                factor_panel[step_index, slot : slot + 1, 0],
                solved,
                step_index,
            )
            following = solve_row(next_slab[0], step_index + 1)
        matrix_rows = eliminate(
            matrix_rows, global_block, factor_panel[step_index, :, 0], solved, step_index
        )
        if step_index + 1 < STEPS:
            solved = following
    stacked = jnp.concatenate(solved_list, 0)
    depth = stacked.shape[0]
    owners_count = col_count // row_count
    gathered = lax.all_gather(
        stacked.reshape(depth, blocks_cols, 1, width), "col", axis=2, tiled=True
    )
    gathered = gathered.reshape(depth, blocks_cols, owners_count, row_count, width)
    chosen = lax.dynamic_index_in_dim(gathered, row_index, 3, keepdims=False)
    row_panels = chosen.reshape(depth, blocks_rows * width)
    gram = lax.dot_general(
        row_panels, stacked, (((0,), (0,)), ((), ())), precision=lax.Precision.HIGHEST
    )
    gram = (gram * (1.0 / (STEPS * BLK))).reshape(blocks_rows, 1, width, blocks_cols, 1, width)
    finished_count = (K + STEPS) // row_count
    finished = matrix_rows[:finished_count].reshape(finished_count, 1, width, 1, row_count, -1)
    moved = lax.all_to_all(finished, "row", split_axis=4, concat_axis=1, tiled=True)
    return (gram, moved)


def solution(mesh):
    placed = (P(None, "row", None, None, "col", None), P(None, None, "row", None, None))
    return jax.shard_map(
        per_device,
        mesh=mesh,
        in_specs=placed,
        out_specs=(
            P(None, "row", None, None, "col", None),
            P(None, None, None, "col", "row", None),
        ),
        check_vma=False,
    )
```

profile of v0, /device:TPU:1, one launch (start us, length us, event | category | flops | bytes accessed | tf_op | source)
XLA Modules:
  0.0 434.1 jit_solution(2634957382837194387)
XLA Ops:
  7.2 1.1 fusion.16
  8.4 3.8 while.4
  8.4 0.6 fusion.36
  9.0 1.3 bitcast_dynamic-update-slice_fusion.4
  10.3 0.6 fusion.36
  10.9 1.3 bitcast_dynamic-update-slice_fusion.4
  12.2 19.7 %custom-call.4 = f32[2,128,128]{1,2,0:T(8,128)S(1)} custom-call(f32[2,128,128]{2,1,0:T(8,128)S(1)} %get-tuple-element.17), custom_call_target="InvertDiagBlocksLowerTriangular" | custom-call | tf_op jit(solution)/shard_map/triangular_solve/custom-call.1 | solution.py:30
  31.9 4.2 slice_reduce_fusion
  36.3 0.6 fusion.13
  36.9 0.6 convolution_subtract_fusion.1
  37.5 0.6 fusion.22
  38.1 1.0 pad_maximum_fusion.1
  39.2 0.6 all-gather.10.cloned.1.call-start
  39.8 0.6 slice.46
  41.7 0.5 slice.47
  42.2 4.1 while.5
  42.2 0.7 fusion.37
  42.9 1.3 bitcast_dynamic-update-slice_fusion.5
  44.3 0.7 fusion.37
  44.9 1.3 bitcast_dynamic-update-slice_fusion.5
  46.3 19.7 %custom-call.5 = f32[2,128,128]{1,2,0:T(8,128)S(1)} custom-call(f32[2,128,128]{2,1,0:T(8,128)S(1)} %get-tuple-element.18), custom_call_target="InvertDiagBlocksLowerTriangular" | custom-call | tf_op jit(solution)/shard_map/triangular_solve/custom-call.1 | solution.py:30
  66.0 27.0 %all-gather.8.cloned.1.call-done = f32[2048,1024]{1,0:T(8,128)} async-done(((f32[256,1024]{1,0:T(8,128)}), f32[2048,1024]{1,0:T(8,128)}) %all-gather.8.cloned.1.call-update) | async-done | bytes 8388624 | tf_op jit(solution)/shard_map/all_gather | solution.py:12
  93.0 2.9 fusion.8
  95.8 0.6 fusion.11
  96.5 0.6 convolution_subtract_fusion
  97.1 0.6 fusion.20
  97.7 1.0 pad_maximum_fusion.2
  99.0 1.3 slice.86
  100.3 0.5 concatenate.13
  100.8 1.2 copy.38
  101.9 47.1 %all-gather.10.cloned.1.call-done = f32[2048,1024]{1,0:T(8,128)} async-done(((f32[256,1024]{1,0:T(8,128)}), f32[2048,1024]{1,0:T(8,128)}) %all-gather.10.cloned.1.call-update) | async-done | bytes 8388624 | tf_op jit(solution)/shard_map/all_gather | solution.py:12
  149.1 1.3 slice.92
  151.1 2.8 pad_maximum_fusion
  153.9 20.9 %copy.42 = f32[8,1,256,4,1,256]{2,5,3,0,4,1:T(8,128)} copy(f32[8,1,256,4,1,256]{5,4,3,2,1,0:T(1,128)} %param.4) | data formatting | bytes 16777216 | tf_op args[0]
  175.1 17.2 %convolution_bitcast_fusion.1 = f32[8,256,1024]{1,2,0:T(8,128)} fusion(f32[2,8,1,256,256]{4,3,1,2,0:T(8,128)} %bitcast.110, f32[2048,1024]{1,0:T(8,128)} %all-gather.8.cloned.1.call-done), kind=kOutput, calls=%fused_computation.11 | convolution fusion | flops 6442450944 | bytes 11534336 | tf_op jit(solution)/shard_map/rab,bc->rac/dot_general | solution.py:35
  192.3 1.3 copy.48
  193.6 16.5 %convolution_bitcast_fusion = f32[8,256,1024]{1,2,0:T(8,128)S(1)} fusion(f32[2,8,1,256,256]{4,3,1,2,0:T(8,128)} %bitcast.111, f32[2048,1024]{1,0:T(8,128)} %all-gather.10.cloned.1.call-done), kind=kOutput, calls=%fused_computation.10 | convolution fusion | flops 6442450944 | bytes 11534336 | tf_op jit(solution)/shard_map/rab,bc->rac/dot_general | solution.py:35
  210.2 4.9 %fusion = f32[4,256,1024]{1,2,0:T(8,128)} fusion(f32[8,256,1024]{1,2,0:T(8,128)S(1)} %convolution_bitcast_fusion, f32[8,256,1024]{1,2,0:T(8,128)S(1)} %copy-done, f32[8,256,1024]{1,2,0:T(8,128)} %bitcast.108, f32[256,1024]{0,1:T(8,128)S(1)} %copy-done.1, f32[256,1024]{0,1:T(8,128)S(1)} %copy.45, pred[4]{0:T(512)(128)(4,1)S(1)} %bitcast.117, ...), kind=kLoop, calls=%fused_computation.7 | loop fusion | flops 6291456 | bytes 18874384 | tf_op jit(solution)/shard_map/jit(_where)/select_n | solution.py:40
  215.1 5.7 %copy.49 = f32[4,1,256,1,8,128]{5,2,0,3,1,4:T(8,128)} copy(f32[4,1,256,1,8,128]{2,5,4,0,3,1:T(8,128)} %bitcast.109) | data formatting | bytes 8388608 | tf_op jit(solution)/shard_map/reshape | solution.py:75
  220.9 4.7 %all-to-all-start = ((f32[4,1,256,1,8,128]{5,2,0,3,1,4:T(8,128)}), f32[4,1,256,1,8,128]{5,2,0,3,1,4:T(8,128)}, u32[]{:S(2)}, u32[]{:S(2)}) async-start(f32[4,1,256,1,8,128]{5,2,0,3,1,4:T(8,128)} %copy.49), calls=%async_computation | async-start | bytes 8388608 | tf_op jit(solution)/shard_map/all_to_all | solution.py:76
  225.5 48.9 %all-to-all-done = f32[4,1,256,1,8,128]{5,2,0,3,1,4:T(8,128)} async-done(((f32[4,1,256,1,8,128]{5,2,0,3,1,4:T(8,128)}), f32[4,1,256,1,8,128]{5,2,0,3,1,4:T(8,128)}, u32[]{:S(2)}, u32[]{:S(2)}) %all-to-all-start) | async-done | bytes 4194336 | tf_op jit(solution)/shard_map/all_to_all | solution.py:76
  274.5 11.4 %copy.51 = f32[4,8,256,1,1,128]{5,4,3,2,1,0:T(1,128)} copy(f32[4,8,256,1,1,128]{5,2,0,1,4,3:T(8,128)} %bitcast.26) | data formatting | bytes 8388608
  285.8 64.7 %all-gather.6.cloned.1.call-done = f32[512,4,16,256]{3,0,1,2:T(8,128)} async-done(((f32[512,4,1,256]{3,0,1,2:T(8,128)}), f32[512,4,16,256]{3,0,1,2:T(8,128)}) %all-gather.6.cloned.1.call-update) | async-done | bytes 33554448 | tf_op jit(solution)/shard_map/all_gather | solution.py:64
  350.6 28.3 %copy.59 = f32[512,4,16,256]{3,2,1,0:T(8,128)S(1)} copy(f32[512,4,16,256]{3,0,1,2:T(8,128)} %all-gather.6.cloned.1.call-done) | data formatting | bytes 67108864 | tf_op jit(solution)/shard_map/all_gather | solution.py:64
  378.8 6.6 %constant_dynamic-slice_fusion.2 = f32[512,4,2,1,256]{4,3,2,1,0:T(1,128)} fusion(f32[512,4,2,8,256]{4,3,2,1,0:T(8,128)S(1)} %bitcast.106, s32[]{:T(128)S(6)} %select_n.57), kind=kLoop, calls=%fused_computation.59 | loop fusion | bytes 8388612 | tf_op jit(solution)/shard_map/jit(dynamic_index_in_dim)/dynamic_slice | solution.py:68
  385.5 10.9 %copy.41 = f32[512,4,2,1,256]{0,4,2,1,3:T(8,128)} copy(f32[512,4,2,1,256]{4,3,2,1,0:T(1,128)} %constant_dynamic-slice_fusion.2) | data formatting | bytes 8388608 | tf_op jit(solution)/shard_map/jit(dynamic_index_in_dim)/dynamic_slice | solution.py:68
  396.4 17.5 %convolution_multiply_fusion = f32[2048,1024]{1,0:T(8,128)} fusion(f32[512,2048]{0,1:T(8,128)} %bitcast.107, f32[256,1024]{1,0:T(8,128)S(1)} %slice.92, f32[256,1024]{1,0:T(8,128)S(1)} %slice.86), kind=kOutput, calls=%fused_computation.5 | convolution fusion | flops 12887523328 | bytes 14680064 | tf_op jit(solution)/shard_map/dot_general | solution.py:70
  413.9 13.5 %reshape.102 = f32[8,1,256,4,1,256]{5,4,3,2,1,0:T(1,128)} reshape(f32[2048,1024]{1,0:T(8,128)} %convolution_multiply_fusion) | data formatting | bytes 16777216 | tf_op jit(solution)/shard_map/reshape | solution.py:73
  (24 shorter events, 1.7 us)
Async XLA Ops:
  7.2 85.8 %all-gather.8.cloned.1.call-start = ((), (), s32[]{:S(2)}) async-start(), calls=%async_computation.2 | async-start | bytes 9437184 | tf_op jit(solution)/shard_map/all_gather | solution.py:12
  39.2 109.9 %all-gather.10.cloned.1.call-start = ((), (), s32[]{:S(2)}) async-start(), calls=%async_computation.3 | async-start | bytes 9437184 | tf_op jit(solution)/shard_map/all_gather | solution.py:12
  98.8 251.8 %all-gather.6.cloned.1.call-start = ((), (), s32[]{:S(2)}) async-start(), calls=%async_computation.1 | async-start | bytes 35651584 | tf_op jit(solution)/shard_map/all_gather | solution.py:64
  193.6 16.6 %copy-start = (f32[8,256,1024]{1,2,0:T(8,128)S(1)}, f32[8,256,1024]{1,2,0:T(8,128)}, u32[]{:S(2)}) copy-start(f32[8,256,1024]{1,2,0:T(8,128)} %convolution_bitcast_fusion.1) | copy-start | bytes 25165828
  193.6 16.6 %copy-start.1 = (f32[256,1024]{0,1:T(8,128)S(1)}, f32[256,1024]{0,1:T(8,128)}, u32[]{:S(2)}) copy-start(f32[256,1024]{0,1:T(8,128)} %copy.48) | copy-start | bytes 3145732
  220.9 53.6 %all-to-all-start = ((f32[4,1,256,1,8,128]{5,2,0,3,1,4:T(8,128)}), f32[4,1,256,1,8,128]{5,2,0,3,1,4:T(8,128)}, u32[]{:S(2)}, u32[]{:S(2)}) async-start(f32[4,1,256,1,8,128]{5,2,0,3,1,4:T(8,128)} %copy.49), calls=%async_computation | async-start | bytes 8388608 | tf_op jit(solution)/shard_map/all_to_all | solution.py:76
Sparse Core Ops, SparseCore 0:
  39.3 53.6 all-gather.7
  98.9 50.1 all-gather.9
  154.0 196.5 all-gather.5
where the time goes:
time: 441 us; the launch traced here: 434 us
  waiting for transfers between devices  188 us (43%)
  local copies, waits for them, and re-layouts  117 us (27%)
  matrix products  57.8 us (13%)
  other arithmetic  50.2 us (11%)
  between operations  15.5 us (4%)
  starting transfers between devices  5.49 us (1%)
    all_gather x2, waiting for transfers between devices, picked(): lax.all_gather(value, axis)  74.1 us
    all_gather x1, waiting for transfers between devices, per_device(): lax.all_gather(stacked.reshape(depth, blocks_cols, 1, width), 'col', axis...  64.7 us
    all_to_all x1, waiting for transfers between devices, per_device(): lax.all_to_all(finished, 'row', split_axis=4, concat_axis=1, tiled=True)  48.9 us
    another operation x6, other arithmetic, solve_row(): lax.linalg.triangular_solve(diagonal, slab, left_side=True, lower=True)  42.5 us
    dot_general x3, matrix products, eliminate(): jnp.einsum('rab,bc->rac', column_part, solved, precision=lax.Precision.HI...  36.6 us
    unnamed x7, local copies, waits for them, and re-layouts  32.5 us
    all_gather x1, local copies, waits for them, and re-layouts, per_device(): lax.all_gather(stacked.reshape(depth, blocks_cols, 1, width), 'col', axis...  28.3 us
    dynamic_slice x2, local copies, waits for them, and re-layouts, per_device(): chosen = lax.dynamic_index_in_dim(gathered, row_index, 3, keepdims=False)  17.6 us
  transfers between devices with their start and end apart: 4, of which 4 were waited for; matrix products, arithmetic and copies ran while one was open for 24% of the time, Pallas kernels for 0%

commit v1 on v0

--- a/solution.py
+++ b/solution.py
@@ -61,8 +61,14 @@
     stacked = jnp.concatenate(solved_list, 0)
     depth = stacked.shape[0]
     owners_count = col_count // row_count
-    gathered = lax.all_gather(
-        stacked.reshape(depth, blocks_cols, 1, width), "col", axis=2, tiled=True
+    gathered = jnp.concatenate(
+        lax.all_to_all(
+            jnp.stack([stacked.reshape(depth, blocks_cols, 1, width)] * lax.axis_size("col")),
+            "col",
+            0,
+            0,
+        ),
+        axis=2,
     )
     gathered = gathered.reshape(depth, blocks_cols, owners_count, row_count, width)
     chosen = lax.dynamic_index_in_dim(gathered, row_index, 3, keepdims=False)

time: 441 us -> 843 us (1.91)
  waiting for transfers between devices: 188 us -> 570 us
  local copies, waits for them, and re-layouts: 117 us -> 128 us
    all_to_all x0 -> x1, waiting for transfers between devices: none -> 489 us  [per_device(): lax.all_to_all(jnp.stack([stacked.reshape(depth, blocks_cols, 1, width)]...]
    all_gather x1 -> x0, waiting for transfers between devices: 64.7 us -> none  [per_device(): lax.all_gather(stacked.reshape(depth, blocks_cols, 1, width), 'col', axis...]
    all_gather x2, waiting for transfers between devices: 74.1 us -> 37.8 us  [picked(): lax.all_gather(value, axis)]
    all_gather x1 -> x0, local copies, waits for them, and re-layouts: 28.3 us -> none  [per_device(): lax.all_gather(stacked.reshape(depth, blocks_cols, 1, width), 'col', axis...]
    all_to_all x0 -> x1, local copies, waits for them, and re-layouts: none -> 28.2 us  [per_device(): lax.all_to_all(jnp.stack([stacked.reshape(depth, blocks_cols, 1, width)]...]
    another operation x0 -> x1, local copies, waits for them, and re-layouts: none -> 12.3 us  [per_device(): jnp.stack([stacked.reshape(depth, blocks_cols, 1, width)] * lax.axis_size...]
    unnamed x7 -> x5, local copies, waits for them, and re-layouts: 32.5 us -> 32.2 us
  transfers between devices with their start and end apart: 4 -> 4, of which waited for: 4 -> 4; matrix products, arithmetic and copies ran while one was open for 24% -> 10% of each run, Pallas kernels for 0% -> 0%
where the time goes in v1:
time: 843 us; the launch traced here: 835 us
  waiting for transfers between devices  570 us (68%)
  local copies, waits for them, and re-layouts  128 us (15%)
  matrix products  57.9 us (7%)
  other arithmetic  50.9 us (6%)
  between operations  15.7 us (2%)
  starting transfers between devices  11.9 us (1%)
    all_to_all x1, waiting for transfers between devices, per_device(): lax.all_to_all(jnp.stack([stacked.reshape(depth, blocks_cols, 1, width)]...  489 us
    all_to_all x1, waiting for transfers between devices, per_device(): lax.all_to_all(finished, 'row', split_axis=4, concat_axis=1, tiled=True)  44 us
    another operation x6, other arithmetic, solve_row(): lax.linalg.triangular_solve(diagonal, slab, left_side=True, lower=True)  42.5 us
    all_gather x2, waiting for transfers between devices, picked(): lax.all_gather(value, axis)  37.8 us
    dot_general x3, matrix products, eliminate(): jnp.einsum('rab,bc->rac', column_part, solved, precision=lax.Precision.HI...  36.7 us
    unnamed x5, local copies, waits for them, and re-layouts  32.2 us
    all_to_all x1, local copies, waits for them, and re-layouts, per_device(): lax.all_to_all(jnp.stack([stacked.reshape(depth, blocks_cols, 1, width)]...  28.2 us
    dynamic_slice x2, local copies, waits for them, and re-layouts, per_device(): chosen = lax.dynamic_index_in_dim(gathered, row_index, 3, keepdims=False)  17.6 us
  transfers between devices with their start and end apart: 4, of which 4 were waited for; matrix products, arithmetic and copies ran while one was open for 10% of the time, Pallas kernels for 0%

profile of v1, /device:TPU:1, one launch (start us, length us, event | category | flops | bytes accessed | tf_op | source)
XLA Modules:
  0.0 835.2 jit_solution(3478437176535402484)
XLA Ops:
  7.2 1.1 fusion.16
  8.4 4.0 while.4
  8.4 0.6 fusion.36
  9.0 1.4 bitcast_dynamic-update-slice_fusion.4
  10.4 0.6 fusion.36
  11.0 1.4 bitcast_dynamic-update-slice_fusion.4
  12.4 19.7 %custom-call.4 = f32[2,128,128]{1,2,0:T(8,128)S(1)} custom-call(f32[2,128,128]{2,1,0:T(8,128)S(1)} %get-tuple-element.17), custom_call_target="InvertDiagBlocksLowerTriangular" | custom-call | tf_op jit(solution)/shard_map/triangular_solve/custom-call.1 | solution.py:30
  32.0 4.2 slice_reduce_fusion
  36.4 0.6 fusion.13
  37.0 0.6 convolution_subtract_fusion.1
  37.6 0.6 fusion.22
  38.3 1.0 pad_maximum_fusion
  39.3 0.6 all-gather.7.cloned.1.call-start
  39.9 0.6 slice.46
  42.4 3.8 while.5
  42.4 0.6 fusion.37
  43.0 1.3 bitcast_dynamic-update-slice_fusion.5
  44.3 0.6 fusion.37
  44.9 1.3 bitcast_dynamic-update-slice_fusion.5
  46.2 19.7 %custom-call.5 = f32[2,128,128]{1,2,0:T(8,128)S(1)} custom-call(f32[2,128,128]{2,1,0:T(8,128)S(1)} %get-tuple-element.18), custom_call_target="InvertDiagBlocksLowerTriangular" | custom-call | tf_op jit(solution)/shard_map/triangular_solve/custom-call.1 | solution.py:30
  65.9 27.3 %all-gather.5.cloned.1.call-done = f32[2048,1024]{1,0:T(8,128)} async-done(((f32[256,1024]{1,0:T(8,128)}), f32[2048,1024]{1,0:T(8,128)}) %all-gather.5.cloned.1.call-update) | async-done | bytes 8388624 | tf_op jit(solution)/shard_map/all_gather | solution.py:12
  93.2 2.9 fusion.8
  96.1 0.6 fusion.11
  96.7 0.6 convolution_subtract_fusion
  97.3 0.6 fusion.20
  97.9 1.0 pad_maximum_fusion.1
  99.0 20.8 %copy.38 = f32[8,1,256,4,1,256]{2,5,3,0,4,1:T(8,128)} copy(f32[8,1,256,4,1,256]{5,4,3,2,1,0:T(1,128)} %param.4) | data formatting | bytes 16777216 | tf_op args[0]
  119.8 1.3 slice.86
  121.5 17.4 %convolution_bitcast_fusion.1 = f32[8,256,1024]{1,2,0:T(8,128)} fusion(f32[2,8,1,256,256]{4,3,1,2,0:T(8,128)} %bitcast.114, f32[2048,1024]{1,0:T(8,128)} %all-gather.5.cloned.1.call-done), kind=kOutput, calls=%fused_computation.11 | convolution fusion | flops 6442450944 | bytes 11534336 | tf_op jit(solution)/shard_map/rab,bc->rac/dot_general | solution.py:35
  138.8 10.5 %all-gather.7.cloned.1.call-done = f32[2048,1024]{1,0:T(8,128)} async-done(((f32[256,1024]{1,0:T(8,128)}), f32[2048,1024]{1,0:T(8,128)}) %all-gather.7.cloned.1.call-update) | async-done | bytes 8388624 | tf_op jit(solution)/shard_map/all_gather | solution.py:12
  149.4 1.3 slice.92
  150.7 1.3 copy.44
  152.0 16.5 %convolution_bitcast_fusion = f32[8,256,1024]{1,2,0:T(8,128)S(1)} fusion(f32[2,8,1,256,256]{4,3,1,2,0:T(8,128)} %bitcast.115, f32[2048,1024]{1,0:T(8,128)} %all-gather.7.cloned.1.call-done), kind=kOutput, calls=%fused_computation.10 | convolution fusion | flops 6442450944 | bytes 11534336 | tf_op jit(solution)/shard_map/rab,bc->rac/dot_general | solution.py:35
  168.5 5.4 fusion
  173.8 5.3 copy.45
  179.1 4.7 all-to-all-start.1
  184.3 1.5 concatenate.14
  185.8 3.0 maximum_bitcast_fusion
  188.8 44.0 %all-to-all-done.1 = f32[4,1,256,1,8,128]{5,2,0,3,1,4:T(8,128)} async-done(((f32[4,1,256,1,8,128]{5,2,0,3,1,4:T(8,128)}), f32[4,1,256,1,8,128]{5,2,0,3,1,4:T(8,128)}, u32[]{:S(2)}, u32[]{:S(2)}) %all-to-all-start.1) | async-done | bytes 4194336 | tf_op jit(solution)/shard_map/all_to_all | solution.py:82
  232.7 12.3 %stack.3 = f32[16,512,4,1,256]{4,2,1,3,0:T(4,128)} broadcast(f32[512,4,256]{2,1,0:T(4,128)} %maximum_bitcast_fusion), dimensions={1,2,4} | broadcast | bytes 35651584 | tf_op jit(solution)/shard_map/stack | solution.py:66
  245.1 6.6 all-to-all-start
  251.7 11.2 %copy.47 = f32[4,8,256,1,1,128]{5,4,3,2,1,0:T(1,128)} copy(f32[4,8,256,1,1,128]{5,2,0,1,4,3:T(8,128)} %bitcast.28) | data formatting | bytes 8388608
  262.9 488.5 %all-to-all-done = f32[16,512,4,1,256]{4,2,1,3,0:T(4,128)} async-done(((f32[16,512,4,1,256]{4,2,1,3,0:T(4,128)}), f32[16,512,4,1,256]{4,2,1,3,0:T(4,128)}, u32[]{:S(2)}, u32[]{:S(2)}) %all-to-all-start) | async-done | bytes 33554464 | tf_op jit(solution)/shard_map/all_to_all | solution.py:65
  751.4 28.2 %copy.55 = f32[16,512,4,1,256]{4,0,2,1,3:T(8,128)S(1)} copy(f32[16,512,4,1,256]{4,2,1,3,0:T(4,128)} %all-to-all-done) | data formatting | bytes 67108864 | tf_op jit(solution)/shard_map/all_to_all | solution.py:65
  779.6 6.6 constant_dynamic-slice_fusion.2
  786.3 10.9 %copy.37 = f32[512,4,2,1,256]{0,4,2,1,3:T(8,128)} copy(f32[512,4,2,1,256]{4,3,2,1,0:T(1,128)} %constant_dynamic-slice_fusion.2) | data formatting | bytes 8388608 | tf_op jit(solution)/shard_map/jit(dynamic_index_in_dim)/dynamic_slice | solution.py:74
  797.2 17.5 %convolution_multiply_fusion = f32[2048,1024]{1,0:T(8,128)} fusion(f32[512,2048]{0,1:T(8,128)} %bitcast.111, f32[256,1024]{1,0:T(8,128)S(1)} %slice.92, f32[256,1024]{1,0:T(8,128)S(1)} %slice.86), kind=kOutput, calls=%fused_computation.5 | convolution fusion | flops 12887523328 | bytes 14680064 | tf_op jit(solution)/shard_map/dot_general | solution.py:76
  814.7 13.5 %reshape.104 = f32[8,1,256,4,1,256]{5,4,3,2,1,0:T(1,128)} reshape(f32[2048,1024]{1,0:T(8,128)} %convolution_multiply_fusion) | data formatting | bytes 16777216 | tf_op jit(solution)/shard_map/reshape | solution.py:79
  (20 shorter events, 1.8 us)
Async XLA Ops:
  7.2 86.0 %all-gather.5.cloned.1.call-start = ((), (), s32[]{:S(2)}) async-start(), calls=%async_computation.2 | async-start | bytes 9437184 | tf_op jit(solution)/shard_map/all_gather | solution.py:12
  39.3 110.0 %all-gather.7.cloned.1.call-start = ((), (), s32[]{:S(2)}) async-start(), calls=%async_computation.3 | async-start | bytes 9437184 | tf_op jit(solution)/shard_map/all_gather | solution.py:12
  152.0 16.5 %copy-start = (f32[256,1024]{0,1:T(8,128)S(1)}, f32[256,1024]{0,1:T(8,128)}, u32[]{:S(2)}) copy-start(f32[256,1024]{0,1:T(8,128)} %copy.44) | copy-start | bytes 3145732
  179.1 53.6 %all-to-all-start.1 = ((f32[4,1,256,1,8,128]{5,2,0,3,1,4:T(8,128)}), f32[4,1,256,1,8,128]{5,2,0,3,1,4:T(8,128)}, u32[]{:S(2)}, u32[]{:S(2)}) async-start(f32[4,1,256,1,8,128]{5,2,0,3,1,4:T(8,128)} %copy.45), calls=%async_computation.1 | async-start | bytes 8388608 | tf_op jit(solution)/shard_map/all_to_all | solution.py:82
  245.1 506.3 %all-to-all-start = ((f32[16,512,4,1,256]{4,2,1,3,0:T(4,128)}), f32[16,512,4,1,256]{4,2,1,3,0:T(4,128)}, u32[]{:S(2)}, u32[]{:S(2)}) async-start(f32[16,512,4,1,256]{4,2,1,3,0:T(4,128)} %stack.3), calls=%async_computation | async-start | bytes 67108864 | tf_op jit(solution)/shard_map/all_to_all | solution.py:65
Sparse Core Ops, SparseCore 0:
  39.5 53.6 all-gather.4
  99.1 50.1 all-gather.6
